TPU v7x, 128 devices: a whole 4x4x4 slice. The times are simulated.
128 devices in a mesh: row: 8 (over x, core), col: 16 (over z, y).
Axes of the slice: x: 4, y: 4, z: 4, core: 2. Of those that a mesh axis runs over, the one named last changes fastest.
Arguments:
- pair_in: bfloat16 [512, 512, 128], P('row', 'col'), may hold values from -6 to 6
- proj_weight: bfloat16 [2, 128, 512], replicated, may hold values from -0.5 to 0.5
- gate_weight: bfloat16 [2, 128, 128], replicated, may hold values from -0.5 to 0.5
- out_weight: bfloat16 [2, 128, 128], replicated, may hold values from -0.5 to 0.5
- block_mask: int32 [4, 4], replicated, may hold values 0 or 1
Outputs:
- pair_out: bfloat16 [512, 512, 128], P('row', 'col')
Inputs may be any that keep to these rules, and one draw needn't show every extreme that they name: `block_mask`: 1 marks an active chain-pair block of 128 x 128 tokens, 0 an inactive one.
All inputs are finite; a program needn't handle non-finite values.
Results may differ from a plain program's by a relative error of at most 0.01.
Values may be sent and summed in bfloat16 or wider, within the bound.
A program may use at most 64 MiB of HBM per device.

v0:
```python
import jax
import jax.numpy as jnp
from jax import lax
from jax.experimental import pallas as pl
from jax.experimental.pallas import tpu as pltpu
from jax.sharding import PartitionSpec as P

MESH = pl.DeviceIdType.MESH
F32 = jnp.float32
BF16 = jnp.bfloat16
EPS = 1e-5

ROWS, COLS = 8, 16
DEVICES = ROWS * COLS
N = 512
C = 128
RI, CJ = 64, 32
JH = 16
TOK = RI * CJ
GROUPS = 4
GCH = DEVICES // GROUPS


def sigmoid(v):
    return 0.5 * jnp.tanh(0.5 * v) + 0.5


def norm_rows(v):
    center = v - jnp.mean(v, axis=0, keepdims=True)
    var = jnp.mean(center * center, axis=0, keepdims=True)
    return center * lax.rsqrt(var + EPS)


def coords(dst):
    return {"row": dst // COLS, "col": dst % COLS}


def kernel(
    pair_ref, wp_ref, wg_ref, wo_ref, mask_ref, out_ref,
    xf, pt, nt, gate, wpt, wgt, wot, fbuf, gbuf, mat, tri,
    s_lr0, s_lr1, r_lr0, r_lr1, s_t0, s_t1, r_t0, r_t1,
    send_sem, recv_sem,
):
    row, col = lax.axis_index("row"), lax.axis_index("col")
    me = row * COLS + col
    barrier = pltpu.get_barrier_semaphore()

    def greet(s, carry):
        dst = (me + s) % DEVICES
        pl.semaphore_signal(barrier, inc=1, device_id=coords(dst), device_id_type=MESH)
        return carry

    lax.fori_loop(1, DEVICES, greet, 0)

    mask = mask_ref[row // 2, col // 4].astype(F32)
    sends = ((s_lr0, s_t0), (s_lr1, s_t1))
    recvs = ((r_lr0, r_t0), (r_lr1, r_t1))

    def prepare_weights(t):
        for kind in range(4):
            w = wp_ref[t, :, kind * C : (kind + 1) * C].astype(F32).T.astype(BF16)
            for g in range(GROUPS):
                wpt[g, kind * GCH : (kind + 1) * GCH, :] = w[g * GCH : (g + 1) * GCH]
        wgt[...] = wg_ref[t].astype(F32).T.astype(BF16)
        wot[...] = wo_ref[t].astype(F32).T.astype(BF16)

    def send(t, what, dst):
        src, land = sends[t][what], recvs[t][what]
        pltpu.make_async_remote_copy(
            src_ref=src.at[dst],
            dst_ref=land.at[me],
            send_sem=send_sem.at[t, what],
            recv_sem=recv_sem.at[t, what],
            device_id=coords(dst),
            device_id_type=MESH,
        ).start()

    def wait(t, what, sem):
        land = recvs[t][what].at[pl.ds(0, DEVICES - 1)]
        pltpu.make_async_copy(land, land, sem.at[t, what]).wait()

    def project_and_send(t):
        src, land = sends[t][0], recvs[t][0]

        def group(step, carry):
            g = (step + row // 2 + col // 4 + col) % GROUPS
            w = wpt[g]
            for q in range(TOK // 256):
                v = jnp.dot(w, nt[:, q * 256 : (q + 1) * 256], preferred_element_type=F32)
                for side in range(2):
                    value = v[2 * side * GCH : (2 * side + 1) * GCH]
                    gates = v[(2 * side + 1) * GCH : (2 * side + 2) * GCH]
                    proj = mask * sigmoid(gates) * value
                    for half in range(2):
                        at = side * GCH * JH + 2 * q + half
                        fbuf[pl.ds(at, GCH, stride=JH), :] = proj[:, half * 128 : (half + 1) * 128]
            for side in range(2):
                tiles = fbuf[side * GCH * JH : (side + 1) * GCH * JH, :].astype(BF16)
                src[pl.ds(g * GCH, GCH), side] = tiles.reshape(GCH, JH, 128)

            def one(d, c):
                dst = g * GCH + (d + me) % GCH

                @pl.when(dst != me)
                def _():
                    send(t, 0, dst)

                return c

            lax.fori_loop(0, GCH, one, 0)
            return carry

        lax.fori_loop(0, GROUPS, group, 0)
        land[me] = src[me]

    def gates_of(t):
        for q in range(TOK // 256):
            sl = slice(q * 256, (q + 1) * 256)
            gate[:, sl] = mask * sigmoid(jnp.dot(wgt[...], nt[:, sl], preferred_element_type=F32))

    def triangle_and_send(t):
        land = recvs[t][0]
        src, back = sends[t][1], recvs[t][1]

        def relayout(c, carry):
            for side in range(2):
                for x in range(4):
                    a = land[(2 * x) * COLS + c, side]
                    b = land[(2 * x + 1) * COLS + c, side]
                    low = jnp.concatenate([a[:, :64], b[:, :64]], axis=1)
                    high = jnp.concatenate([a[:, 64:], b[:, 64:]], axis=1)
                    mat[side, pl.ds(c * CJ, JH), x * 128 : (x + 1) * 128] = low
                    mat[side, pl.ds(c * CJ + JH, JH), x * 128 : (x + 1) * 128] = high
            return carry

        lax.fori_loop(0, COLS, relayout, 0)
        for zj in range(4):
            js = slice(zj * 128, (zj + 1) * 128)
            if t == 0:
                v = lax.dot_general(mat[1, :, js], mat[0], (((0,), (0,)), ((), ())), preferred_element_type=F32)
            else:
                v = lax.dot_general(mat[1, js, :], mat[0], (((1,), (1,)), ((), ())), preferred_element_type=F32)
            tri[js, :] = v.astype(BF16)

        def chunk(step, carry):
            z = (step + row // 2 + col // 4 + col) % 4
            for y in range(4):
                c = z * 4 + y
                for x in range(4):
                    a = tri[pl.ds(c * CJ, JH), x * 128 : (x + 1) * 128]
                    b = tri[pl.ds(c * CJ + JH, JH), x * 128 : (x + 1) * 128]
                    src[(2 * x) * COLS + c] = jnp.concatenate([a[:, :64], b[:, :64]], axis=1)
                    src[(2 * x + 1) * COLS + c] = jnp.concatenate([a[:, 64:], b[:, 64:]], axis=1)

            def one(d, cc):
                e = (d + me) % 32
                dst = (e // 4) * COLS + z * 4 + e % 4

                @pl.when(dst != me)
                def _():
                    send(t, 1, dst)

                return cc

            lax.fori_loop(0, 32, one, 0)
            return carry

        lax.fori_loop(0, 4, chunk, 0)
        back[me] = src[me]

    def finish(t):
        back = recvs[t][1]

        def total(h, acc):
            return acc + back[h].astype(F32)

        mean = lax.fori_loop(0, DEVICES, total, jnp.zeros((JH, 128), F32), unroll=8) * (1.0 / DEVICES)

        def square(h, acc):
            d = back[h].astype(F32) - mean
            return acc + d * d

        var = lax.fori_loop(0, DEVICES, square, jnp.zeros((JH, 128), F32), unroll=8) * (1.0 / DEVICES)
        rstd = lax.rsqrt(var + EPS)

        def scale(h, carry):
            gbuf[pl.ds(pl.multiple_of(h * JH, JH), JH), :] = (back[h].astype(F32) - mean) * rstd
            return carry

        lax.fori_loop(0, DEVICES, scale, 0, unroll=8)
        for j in range(JH):
            sl = slice(j * 128, (j + 1) * 128)
            tn = gbuf[pl.ds(j, DEVICES, stride=JH), :].astype(BF16)
            update = jnp.dot(wot[...], tn, preferred_element_type=F32)
            new = (pt[:, sl] + gate[:, sl] * update).astype(BF16).astype(F32)
            if t == 0:
                pt[:, sl] = new
                nt[:, sl] = norm_rows(new).astype(BF16)
            else:
                back_t = new.T
                xf[pl.ds(j, RI, stride=CJ), :] = back_t[:RI]
                xf[pl.ds(j + JH, RI, stride=CJ), :] = back_t[RI:]

    xf[...] = pair_ref[...].reshape(TOK, C).astype(F32)
    for j in range(JH):
        sl = slice(j * 128, (j + 1) * 128)
        tokens = jnp.concatenate(
            [xf[pl.ds(j, RI, stride=CJ), :], xf[pl.ds(j + JH, RI, stride=CJ), :]], axis=0
        )
        v = tokens.T
        pt[:, sl] = v
        nt[:, sl] = norm_rows(v).astype(BF16)
    prepare_weights(0)
    pl.semaphore_wait(barrier, DEVICES - 1)
    for t in range(2):
        project_and_send(t)
        gates_of(t)
        wait(t, 0, recv_sem)
        triangle_and_send(t)
        wait(t, 1, recv_sem)
        finish(t)
        if t == 0:
            prepare_weights(1)
    for t in range(2):
        for what in range(2):
            wait(t, what, send_sem)
    out_ref[...] = xf[...].astype(BF16).reshape(RI, CJ, C)


def on_device(pair_in, proj_weight, gate_weight, out_weight, block_mask):
    lr = pltpu.VMEM((DEVICES, 2, JH, 128), BF16)
    tr = pltpu.VMEM((DEVICES, JH, 128), BF16)
    vmem = pl.BlockSpec(memory_space=pltpu.VMEM)
    return pl.pallas_call(
        kernel,
        out_shape=jax.ShapeDtypeStruct((RI, CJ, C), BF16),
        in_specs=[vmem, vmem, vmem, vmem, pl.BlockSpec(memory_space=pltpu.SMEM)],
        out_specs=vmem,
        scratch_shapes=[
            pltpu.VMEM((TOK, C), F32),
            pltpu.VMEM((C, TOK), F32),
            pltpu.VMEM((C, TOK), BF16),
            pltpu.VMEM((C, TOK), F32),
            pltpu.VMEM((GROUPS, 4 * GCH, C), BF16),
            pltpu.VMEM((C, C), BF16),
            pltpu.VMEM((C, C), BF16),
            pltpu.VMEM((2 * GCH * JH, 128), F32),
            pltpu.VMEM((DEVICES * JH, 128), F32),
            pltpu.VMEM((2, N, N), BF16),
            pltpu.VMEM((N, N), BF16),
            lr, lr, lr, lr, tr, tr, tr, tr,
            pltpu.SemaphoreType.DMA((2, 2)),
            pltpu.SemaphoreType.DMA((2, 2)),
        ],
        compiler_params=pltpu.CompilerParams(
            collective_id=0, has_side_effects=True, vmem_limit_bytes=40 * 2**20
        ),
        name="triangle_pair",
    )(pair_in, proj_weight, gate_weight, out_weight, block_mask)


def solution(mesh):
    placed = (P("row", "col", None), P(), P(), P(), P())
    return jax.shard_map(
        on_device, mesh=mesh, in_specs=placed, out_specs=P("row", "col", None), check_vma=False
    )
```

profile of v0, /device:TPU:1, one launch (start us, length us, event | category | flops | bytes accessed | tf_op | source)
XLA Modules:
  0.0 82.6 jit_solution(552589391369307058)
XLA Ops:
  0.0 0.0 copy-start
  0.0 1.0 %copy-done = bf16[64,32,128]{2,1,0:T(8,128)(2,1)S(1)} copy-done((bf16[64,32,128]{2,1,0:T(8,128)(2,1)S(1)}, bf16[64,32,128]{2,1,0:T(8,128)(2,1)}, u32[]{:S(2)}) %copy-start) | copy-done | bytes 524312
  1.0 0.0 copy-start.1
  1.0 0.9 %copy-done.1 = bf16[2,128,512]{2,1,0:T(8,128)(2,1)S(1)} copy-done((bf16[2,128,512]{2,1,0:T(8,128)(2,1)S(1)}, bf16[2,128,512]{2,1,0:T(8,128)(2,1)}, u32[]{:S(2)}) %copy-start.1) | copy-done | bytes 262168
  2.0 0.0 copy-start.2
  2.0 0.8 %copy-done.2 = bf16[2,128,128]{2,1,0:T(8,128)(2,1)S(1)} copy-done((bf16[2,128,128]{2,1,0:T(8,128)(2,1)S(1)}, bf16[2,128,128]{2,1,0:T(8,128)(2,1)}, u32[]{:S(2)}) %copy-start.2) | copy-done | bytes 65560
  2.8 0.0 copy-start.3
  2.8 0.8 %copy-done.3 = bf16[2,128,128]{2,1,0:T(8,128)(2,1)S(1)} copy-done((bf16[2,128,128]{2,1,0:T(8,128)(2,1)S(1)}, bf16[2,128,128]{2,1,0:T(8,128)(2,1)}, u32[]{:S(2)}) %copy-start.3) | copy-done | bytes 65560
  3.7 0.0 copy-start.4
  3.7 0.7 copy-done.4
  4.4 77.4 %triangle_pair.1 = bf16[64,32,128]{2,1,0:T(8,128)(2,1)S(1)} custom-call(bf16[64,32,128]{2,1,0:T(8,128)(2,1)S(1)} %copy-done, bf16[2,128,512]{2,1,0:T(8,128)(2,1)S(1)} %copy-done.1, bf16[2,128,128]{2,1,0:T(8,128)(2,1)S(1)} %copy-done.2, bf16[2,128,128]{2,1,0:T(8,128)(2,1)S(1)} %copy-done.3, s32[4,4]{1,0:T(4,128)S(1)} %copy-done.4), custom_call_target="tpu_custom_call" | custom-call | tf_op jit(solution)/shard_map/triangle_pair/pallas_call | solution.py:234
  81.8 0.8 copy.7
Async XLA Ops:
  0.0 1.0 %copy-start = (bf16[64,32,128]{2,1,0:T(8,128)(2,1)S(1)}, bf16[64,32,128]{2,1,0:T(8,128)(2,1)}, u32[]{:S(2)}) copy-start(bf16[64,32,128]{2,1,0:T(8,128)(2,1)} %pair_ref.1) | copy-start | bytes 1572868
  1.0 0.9 %copy-start.1 = (bf16[2,128,512]{2,1,0:T(8,128)(2,1)S(1)}, bf16[2,128,512]{2,1,0:T(8,128)(2,1)}, u32[]{:S(2)}) copy-start(bf16[2,128,512]{2,1,0:T(8,128)(2,1)} %wp_ref.1) | copy-start | bytes 786436
  2.0 0.8 %copy-start.2 = (bf16[2,128,128]{2,1,0:T(8,128)(2,1)S(1)}, bf16[2,128,128]{2,1,0:T(8,128)(2,1)}, u32[]{:S(2)}) copy-start(bf16[2,128,128]{2,1,0:T(8,128)(2,1)} %wg_ref.1) | copy-start | bytes 196612
  2.8 0.8 %copy-start.3 = (bf16[2,128,128]{2,1,0:T(8,128)(2,1)S(1)}, bf16[2,128,128]{2,1,0:T(8,128)(2,1)}, u32[]{:S(2)}) copy-start(bf16[2,128,128]{2,1,0:T(8,128)(2,1)} %wo_ref.1) | copy-start | bytes 196612
  3.7 0.7 copy-start.4
where the time goes:
time: 82.9 us; the launch traced here: 82.6 us
  Pallas kernels  77.4 us (93%)
  local copies, waits for them, and re-layouts  5.15 us (6%)
    pallas_call x1, Pallas kernels, on_device(): pl.pallas_call(kernel, out_shape=jax.ShapeDtypeStruct((RI, CJ, C), BF16),...  77.4 us
    unnamed x11, local copies, waits for them, and re-layouts  5.15 us

commit v1 on v0

v1 whole, which is shorter than its diff:
```python
import jax
import jax.numpy as jnp
from jax import lax
from jax.experimental import pallas as pl
from jax.experimental.pallas import tpu as pltpu
from jax.sharding import PartitionSpec as P

MESH = pl.DeviceIdType.MESH
F32 = jnp.float32
BF16 = jnp.bfloat16
EPS = 1e-5

ROWS, COLS = 8, 16
DEVICES = ROWS * COLS
N = 512
C = 128
RI, CJ = 64, 32
JH = 16
TOK = RI * CJ
PLANE = COLS
STEPS = 4
AROUND = [((a + b) % 4, a) for b in range(4) for a in range(4)]


def sigmoid(v):
    return 0.5 * jnp.tanh(0.5 * v) + 0.5


def norm_rows(v):
    center = v - jnp.mean(v, axis=0, keepdims=True)
    var = jnp.mean(center * center, axis=0, keepdims=True)
    return center * lax.rsqrt(var + EPS)


def wrap4(v):
    return jnp.where(v >= 4, v - 4, v)


def kernel(
    pair_hbm, wp_hbm, wg_hbm, wo_hbm, mask_ref, out_ref,
    pair_ref, wp_ref, wg_ref, wo_ref,
    xf, pt, nt, gate, wpt, wgt, wot, fbuf, gbuf, mat, tri,
    s_lr0, s_lr1, r_lr0, r_lr1, s_t0, s_t1, r_t0, r_t1,
    send_sem, recv_sem, load_sem,
):
    row, col = lax.axis_index("row"), lax.axis_index("col")
    loads = [
        pltpu.make_async_copy(src, dst, load_sem.at[i])
        for i, (src, dst) in enumerate(
            [(pair_hbm, pair_ref), (wp_hbm, wp_ref), (wg_hbm, wg_ref), (wo_hbm, wo_ref)]
        )
    ]
    for load in loads:
        load.start()
    x, core = row // 2, row % 2
    z, y = col // 4, col % 4
    me = core * 64 + x * COLS + col
    zs = [z if d == 0 else wrap4(z + d) for d in range(4)]
    ys = [y if d == 0 else wrap4(y + d) for d in range(4)]
    cols = {(dz, dy): zs[dz] * 4 + ys[dy] for dz in range(4) for dy in range(4)}
    flip = (z + y) % 2
    barrier = pltpu.get_barrier_semaphore()

    def greet(s, carry):
        r2 = jnp.where(row + s >= ROWS, row + s - ROWS, row + s)
        for dz, dy in AROUND:
            there = {"row": r2, "col": cols[dz, dy]}
            if (dz, dy) == (0, 0):

                @pl.when(s != 0)
                def _():
                    pl.semaphore_signal(barrier, inc=1, device_id=there, device_id_type=MESH)
            else:
                pl.semaphore_signal(barrier, inc=1, device_id=there, device_id_type=MESH)
        return carry

    lax.fori_loop(0, ROWS, greet, 0)

    mask = mask_ref[x, z].astype(F32)
    sends = ((s_lr0, s_t0), (s_lr1, s_t1))
    recvs = ((r_lr0, r_t0), (r_lr1, r_t1))

    def prepare_weights(t):
        for kind in range(4):
            w = wp_ref[t, :, kind * C : (kind + 1) * C].astype(F32).T.astype(BF16)
            for g in range(DEVICES // PLANE):
                wpt[g, kind * PLANE : (kind + 1) * PLANE, :] = w[g * PLANE : (g + 1) * PLANE]
        wgt[...] = wg_ref[t].astype(F32).T.astype(BF16)
        wot[...] = wo_ref[t].astype(F32).T.astype(BF16)

    def planes_of(pair):
        e = (pair + flip) % 2
        return [wrap4(x + e), wrap4(wrap4(x + e) + 2)]

    def send_group(t, what, k, planes):
        src, land = sends[t][what], recvs[t][what]
        for dz, dy in AROUND:
            for x2 in planes:
                c2 = cols[dz, dy]
                slot = k * 64 + x2 * COLS + c2
                copy = pltpu.make_async_remote_copy(
                    src_ref=src.at[slot],
                    dst_ref=land.at[me],
                    send_sem=send_sem.at[t, what],
                    recv_sem=recv_sem.at[t, what],
                    device_id={"row": 2 * x2 + k, "col": c2},
                    device_id_type=MESH,
                )
                if (dz, dy) == (0, 0):
                    pl.when(slot != me)(copy.start)
                else:
                    copy.start()

    def wait(t, what, sem):
        land = recvs[t][what].at[pl.ds(0, DEVICES - 1)]
        pltpu.make_async_copy(land, land, sem.at[t, what]).wait()

    def project_and_send(t):
        src, land = sends[t][0], recvs[t][0]
        size = PLANE * JH

        def group(step, carry):
            k = step // 2
            planes = planes_of(step % 2)
            w = jnp.concatenate([wpt[k * 4 + x2] for x2 in planes], axis=0)
            for q in range(TOK // 256):
                v = jnp.dot(w, nt[:, q * 256 : (q + 1) * 256], preferred_element_type=F32)
                for p in range(2):
                    for side in range(2):
                        at = p * 4 * PLANE + 2 * side * PLANE
                        proj = mask * sigmoid(v[at + PLANE : at + 2 * PLANE]) * v[at : at + PLANE]
                        for half in range(2):
                            to = (2 * p + side) * size + 2 * q + half
                            fbuf[pl.ds(to, PLANE, stride=JH), :] = proj[:, half * 128 : (half + 1) * 128]
            for p in range(2):
                for side in range(2):
                    at = (2 * p + side) * size
                    tiles = fbuf[at : at + size, :].astype(BF16).reshape(PLANE, JH, 128)
                    src[pl.ds(k * 64 + planes[p] * COLS, PLANE), side] = tiles
            send_group(t, 0, k, planes)
            return carry

        lax.fori_loop(0, STEPS, group, 0)
        land[me] = src[me]

    def gates_of(t):
        for q in range(TOK // 256):
            sl = slice(q * 256, (q + 1) * 256)
            gate[:, sl] = mask * sigmoid(jnp.dot(wgt[...], nt[:, sl], preferred_element_type=F32))

    def triangle_and_send(t):
        land = recvs[t][0]
        src, back = sends[t][1], recvs[t][1]

        def relayout(c, carry):
            for side in range(2):
                for x2 in range(4):
                    a = land[x2 * COLS + c, side]
                    b = land[64 + x2 * COLS + c, side]
                    low = jnp.concatenate([a[:, :64], b[:, :64]], axis=1)
                    high = jnp.concatenate([a[:, 64:], b[:, 64:]], axis=1)
                    mat[side, pl.ds(c * CJ, JH), x2 * 128 : (x2 + 1) * 128] = low
                    mat[side, pl.ds(c * CJ + JH, JH), x2 * 128 : (x2 + 1) * 128] = high
            return carry

        lax.fori_loop(0, COLS, relayout, 0, unroll=4)
        for zj in range(4):
            js = slice(zj * 128, (zj + 1) * 128)
            if t == 0:
                v = lax.dot_general(mat[1, :, js], mat[0], (((0,), (0,)), ((), ())), preferred_element_type=F32)
            else:
                v = lax.dot_general(mat[1, js, :], mat[0], (((1,), (1,)), ((), ())), preferred_element_type=F32)
            v = v.astype(BF16)
            for x2 in range(4):
                tri[x2, js, :] = v[:, x2 * 128 : (x2 + 1) * 128]
        for k in range(2):
            lanes = slice(k * 64, (k + 1) * 64)

            def chunk(pair, carry):
                planes = planes_of(pair)
                for x2 in planes:
                    for c in range(COLS):
                        a = tri[x2, c * CJ : c * CJ + JH, lanes]
                        b = tri[x2, c * CJ + JH : (c + 1) * CJ, lanes]
                        src[k * 64 + x2 * COLS + c] = jnp.concatenate([a, b], axis=1)
                send_group(t, 1, k, planes)
                return carry

            lax.fori_loop(0, 2, chunk, 0)
        back[me] = src[me]

    def finish(t):
        back = recvs[t][1]

        def total(h, acc):
            return acc + back[h].astype(F32)

        mean = lax.fori_loop(0, DEVICES, total, jnp.zeros((JH, 128), F32), unroll=8) * (1.0 / DEVICES)

        def square(h, acc):
            d = back[h].astype(F32) - mean
            return acc + d * d

        var = lax.fori_loop(0, DEVICES, square, jnp.zeros((JH, 128), F32), unroll=8) * (1.0 / DEVICES)
        rstd = lax.rsqrt(var + EPS)

        def scale(h, carry):
            gbuf[pl.ds(pl.multiple_of(h * JH, JH), JH), :] = (back[h].astype(F32) - mean) * rstd
            return carry

        lax.fori_loop(0, DEVICES, scale, 0, unroll=8)
        for j in range(JH):
            sl = slice(j * 128, (j + 1) * 128)
            tn = gbuf[pl.ds(j, DEVICES, stride=JH), :].astype(BF16)
            update = jnp.dot(wot[...], tn, preferred_element_type=F32)
            new = (pt[:, sl] + gate[:, sl] * update).astype(BF16).astype(F32)
            if t == 0:
                pt[:, sl] = new
                nt[:, sl] = norm_rows(new).astype(BF16)
            else:
                back_t = new.T
                xf[pl.ds(j, RI, stride=CJ), :] = back_t[:RI]
                xf[pl.ds(j + JH, RI, stride=CJ), :] = back_t[RI:]

    loads[0].wait()
    xf[...] = pair_ref[...].reshape(TOK, C).astype(F32)
    for j in range(JH):
        sl = slice(j * 128, (j + 1) * 128)
        tokens = jnp.concatenate(
            [xf[pl.ds(j, RI, stride=CJ), :], xf[pl.ds(j + JH, RI, stride=CJ), :]], axis=0
        )
        v = tokens.T
        pt[:, sl] = v
        nt[:, sl] = norm_rows(v).astype(BF16)
    for load in loads[1:]:
        load.wait()
    prepare_weights(0)
    pl.semaphore_wait(barrier, DEVICES - 1)
    for t in range(2):
        project_and_send(t)
        gates_of(t)
        wait(t, 0, recv_sem)
        triangle_and_send(t)
        wait(t, 1, recv_sem)
        finish(t)
        if t == 0:
            prepare_weights(1)
    for t in range(2):
        for what in range(2):
            wait(t, what, send_sem)
    out_ref[...] = xf[...].astype(BF16).reshape(RI, CJ, C)


def on_device(pair_in, proj_weight, gate_weight, out_weight, block_mask):
    lr = pltpu.VMEM((DEVICES, 2, JH, 128), BF16)
    tr = pltpu.VMEM((DEVICES, JH, 128), BF16)
    vmem = pl.BlockSpec(memory_space=pltpu.VMEM)
    hbm = pl.BlockSpec(memory_space=pl.ANY)
    return pl.pallas_call(
        kernel,
        out_shape=jax.ShapeDtypeStruct((RI, CJ, C), BF16),
        in_specs=[hbm, hbm, hbm, hbm, pl.BlockSpec(memory_space=pltpu.SMEM)],
        out_specs=vmem,
        scratch_shapes=[
            pltpu.VMEM(pair_in.shape, BF16),
            pltpu.VMEM(proj_weight.shape, BF16),
            pltpu.VMEM(gate_weight.shape, BF16),
            pltpu.VMEM(out_weight.shape, BF16),
            pltpu.VMEM((TOK, C), F32),
            pltpu.VMEM((C, TOK), F32),
            pltpu.VMEM((C, TOK), BF16),
            pltpu.VMEM((C, TOK), F32),
            pltpu.VMEM((DEVICES // PLANE, 4 * PLANE, C), BF16),
            pltpu.VMEM((C, C), BF16),
            pltpu.VMEM((C, C), BF16),
            pltpu.VMEM((4 * PLANE * JH, 128), F32),
            pltpu.VMEM((DEVICES * JH, 128), F32),
            pltpu.VMEM((2, N, N), BF16),
            pltpu.VMEM((4, N, 128), BF16),
            lr, lr, lr, lr, tr, tr, tr, tr,
            pltpu.SemaphoreType.DMA((2, 2)),
            pltpu.SemaphoreType.DMA((2, 2)),
            pltpu.SemaphoreType.DMA((4,)),
        ],
        compiler_params=pltpu.CompilerParams(
            collective_id=0, has_side_effects=True, vmem_limit_bytes=60 * 2**20
        ),
        name="triangle_pair",
    )(pair_in, proj_weight, gate_weight, out_weight, block_mask)


def solution(mesh):
    placed = (P("row", "col", None), P(), P(), P(), P())
    return jax.shard_map(
        on_device, mesh=mesh, in_specs=placed, out_specs=P("row", "col", None), check_vma=False
    )
```

time: 82.9 us -> 66.9 us (0.81)
  Pallas kernels: 77.4 us -> 64.9 us
  local copies, waits for them, and re-layouts: 5.15 us -> 1.87 us
    pallas_call x1, Pallas kernels: 77.4 us -> 64.9 us  [on_device(): pl.pallas_call(kernel, out_shape=jax.ShapeDtypeStruct((RI, CJ, C), BF16),...]
    unnamed x11 -> x1, local copies, waits for them, and re-layouts: 5.15 us -> 1.87 us
where the time goes in v1:
time: 66.9 us; the launch traced here: 66.8 us
  Pallas kernels  64.9 us (97%)
  local copies, waits for them, and re-layouts  1.87 us (3%)
    pallas_call x1, Pallas kernels, on_device(): pl.pallas_call(kernel, out_shape=jax.ShapeDtypeStruct((RI, CJ, C), BF16),...  64.9 us
    unnamed x1, local copies, waits for them, and re-layouts  1.87 us

profile of v1, /device:TPU:1, one launch (start us, length us, event | category | flops | bytes accessed | tf_op | source)
XLA Modules:
  0.0 66.8 jit_solution(4080711950073484874)
XLA Ops:
  0.0 64.9 %triangle_pair.1 = bf16[64,32,128]{2,1,0:T(8,128)(2,1)} custom-call(bf16[64,32,128]{2,1,0:T(8,128)(2,1)} %pair_hbm.1, bf16[2,128,512]{2,1,0:T(8,128)(2,1)} %wp_hbm.1, bf16[2,128,128]{2,1,0:T(8,128)(2,1)} %wg_hbm.1, bf16[2,128,128]{2,1,0:T(8,128)(2,1)} %wo_hbm.1, s32[4,4]{1,0:T(4,128)} %mask_ref.1), custom_call_target="tpu_custom_call" | custom-call | tf_op jit(solution)/shard_map/triangle_pair/pallas_call | solution.py:259
  64.9 1.9 %copy.7 = bf16[64,32,128]{2,1,0:T(8,128)(2,1)} copy(bf16[64,32,128]{2,1,0:T(8,128)(2,1)} %triangle_pair.1) | data formatting | bytes 1048576

commit v2 on v1

v2 whole, which is shorter than its diff:
```python
import jax
import jax.numpy as jnp
from jax import lax
from jax.experimental import pallas as pl
from jax.experimental.pallas import tpu as pltpu
from jax.sharding import PartitionSpec as P

MESH = pl.DeviceIdType.MESH
F32 = jnp.float32
BF16 = jnp.bfloat16
EPS = 1e-5

ROWS, COLS = 8, 16
DEVICES = ROWS * COLS
N = 512
C = 128
RI, CJ = 64, 32
JH = 16
TOK = RI * CJ
PLANE = COLS


def hops(offset):
    return sum(min(d, 4 - d) for d in offset)


HALVES = [
    sorted(
        ((p, (a + b) % 4, a) for b in range(4) for a in range(4) for p in range(2)),
        key=lambda o: -(hop[o[0]] + hops(o[1:])),
    )
    for hop in ((2, 1), (1, 0))
]
IN_PLANE = sorted((((a + b) % 4, a) for b in range(4) for a in range(4)), key=lambda o: -hops(o))
FAR_FIRST = sorted(
    ((a, (a + b) % 4, (a + c) % 4) for b in range(4) for c in range(4) for a in range(4)),
    key=lambda offset: -hops(offset),
)


def sigmoid(v):
    return 0.5 * jnp.tanh(0.5 * v) + 0.5


def norm_rows(v):
    center = v - jnp.mean(v, axis=0, keepdims=True)
    var = jnp.mean(center * center, axis=0, keepdims=True)
    return center * lax.rsqrt(var + EPS)


def wrap4(v):
    return jnp.where(v >= 4, v - 4, v)


def kernel(
    pair_hbm, wp_hbm, wg_hbm, wo_hbm, mask_ref, out_ref,
    pair_ref, wp_ref, wg_ref, wo_ref,
    xf, pt, nt, gate, wpt, wgt, wot, fbuf, gbuf, mat,
    s_lr0, s_lr1, r_lr0, r_lr1, s_t0, s_t1, r_t0, r_t1,
    send_sem, recv_sem, load_sem,
):
    row, col = lax.axis_index("row"), lax.axis_index("col")
    loads = [
        pltpu.make_async_copy(src, dst, load_sem.at[i])
        for i, (src, dst) in enumerate(
            [(pair_hbm, pair_ref), (wp_hbm, wp_ref), (wg_hbm, wg_ref), (wo_hbm, wo_ref)]
        )
    ]
    for load in loads:
        load.start()
    x, core = row // 2, row % 2
    z, y = col // 4, col % 4
    me = core * 64 + x * COLS + col
    xs, zs, ys = ([v if d == 0 else wrap4(v + d) for d in range(4)] for v in (x, z, y))
    cols = {(dz, dy): zs[dz] * 4 + ys[dy] for dz in range(4) for dy in range(4)}
    xa, xb = jnp.where((z + y) % 2 == 0, xs[1], xs[3]), jnp.where((z + y) % 2 == 0, xs[3], xs[1])
    za, zb = jnp.where((x + y) % 2 == 0, zs[1], zs[3]), jnp.where((x + y) % 2 == 0, zs[3], zs[1])
    barrier = pltpu.get_barrier_semaphore()

    for dx, dz, dy in FAR_FIRST:
        for k in range(2):
            row2 = 2 * xs[dx] + (k if dx or dz or dy else 1 - core)
            if (dx, dz, dy) != (0, 0, 0) or k == 0:
                there = {"row": row2, "col": cols[dz, dy]}
                pl.semaphore_signal(barrier, inc=1, device_id=there, device_id_type=MESH)

    mask = mask_ref[x, z].astype(F32)
    sends = ((s_lr0, s_t0), (s_lr1, s_t1))
    recvs = ((r_lr0, r_t0), (r_lr1, r_t1))

    def prepare_weights(t):
        for kind in range(4):
            w = wp_ref[t, :, kind * C : (kind + 1) * C].astype(F32).T.astype(BF16)
            for g in range(DEVICES // PLANE):
                wpt[g, kind * PLANE : (kind + 1) * PLANE, :] = w[g * PLANE : (g + 1) * PLANE]
        wgt[...] = wg_ref[t].astype(F32).T.astype(BF16)
        wot[t] = wo_ref[t].astype(F32).T.astype(BF16)

    def send(t, what, k, x2, c2, own):
        src, land = sends[t][what], recvs[t][what]
        slot = k * 64 + x2 * COLS + c2
        copy = pltpu.make_async_remote_copy(
            src_ref=src.at[slot],
            dst_ref=land.at[me],
            send_sem=send_sem.at[t, what, k],
            recv_sem=recv_sem.at[t, what],
            device_id={"row": 2 * x2 + k, "col": c2},
            device_id_type=MESH,
        )
        if own:
            keep = pltpu.make_async_copy(src.at[slot], land.at[me], send_sem.at[t, what, k])
            pl.when(core != k)(copy.start)
            pl.when(core == k)(keep.start)
        else:
            copy.start()

    def wait_sent(t, what, k):
        src = sends[t][what].at[pl.ds(0, 64)]
        pltpu.make_async_copy(src, src, send_sem.at[t, what, k]).wait()

    def wait_arrived(t, what):
        wait_sent(t, what, core)
        land = recvs[t][what].at[pl.ds(0, DEVICES - 1)]
        pltpu.make_async_copy(land, land, recv_sem.at[t, what]).wait()

    halves = ((xs[2], xa), (xb, xs[0]))

    def project(t, k, half):
        src = sends[t][0]
        size = PLANE * JH
        planes = halves[half]
        w = jnp.concatenate([wpt[k * 4 + x2] for x2 in planes], axis=0)
        for q in range(TOK // 256):
            v = jnp.dot(w, nt[:, q * 256 : (q + 1) * 256], preferred_element_type=F32)
            for p in range(2):
                for side in range(2):
                    at = p * 4 * PLANE + 2 * side * PLANE
                    proj = mask * sigmoid(v[at + PLANE : at + 2 * PLANE]) * v[at : at + PLANE]
                    for half in range(2):
                        to = (2 * p + side) * size + 2 * q + half
                        fbuf[pl.ds(to, PLANE, stride=JH), :] = proj[:, half * 128 : (half + 1) * 128]
        for p in range(2):
            for side in range(2):
                at = (2 * p + side) * size
                tiles = fbuf[at : at + size, :].astype(BF16).reshape(PLANE, JH, 128)
                src[pl.ds(k * 64 + planes[p] * COLS, PLANE), side] = tiles

    def send_half(t, k, half):
        for p, dz, dy in HALVES[half]:
            send(t, 0, k, halves[half][p], cols[dz, dy], (half, p, dz, dy) == (1, 1, 0, 0))

    def gates_of(t):
        for q in range(TOK // 256):
            sl = slice(q * 256, (q + 1) * 256)
            gate[:, sl] = mask * sigmoid(jnp.dot(wgt[...], nt[:, sl], preferred_element_type=F32))

    def triangle_and_send(t):
        land = recvs[t][0]
        src = sends[t][1]

        def relayout(c, carry):
            rows = pl.ds(pl.multiple_of(c * CJ, CJ), JH), pl.ds(pl.multiple_of(c * CJ + JH, JH), JH)
            for side in range(2):
                for x2 in range(4):
                    a = land[x2 * COLS + c, side]
                    b = land[64 + x2 * COLS + c, side]
                    mat[side, x2, rows[0]] = jnp.concatenate([a[:, :64], b[:, :64]], axis=1)
                    mat[side, x2, rows[1]] = jnp.concatenate([a[:, 64:], b[:, 64:]], axis=1)
            return carry

        lax.fori_loop(0, COLS, relayout, 0, unroll=4)
        left = jnp.concatenate([mat[0, x2] for x2 in range(4)], axis=1)
        for dz, z2 in ((2, zs[2]), (1, za), (3, zb), (0, zs[0])):
            if t == 0:
                v = lax.dot_general(mat[1, z2], left, (((0,), (0,)), ((), ())), preferred_element_type=F32)
            else:
                js = pl.ds(pl.multiple_of(z2 * 128, 128), 128)
                right = jnp.concatenate([mat[1, x2, js] for x2 in range(4)], axis=1)
                v = lax.dot_general(right, left, (((1,), (1,)), ((), ())), preferred_element_type=F32)
            v = v.astype(BF16)
            for k in range(2):
                for x2 in range(4):
                    lanes = slice(x2 * 128 + k * 64, x2 * 128 + (k + 1) * 64)
                    for y2 in range(4):
                        a = v[y2 * CJ : y2 * CJ + JH, lanes]
                        b = v[y2 * CJ + JH : (y2 + 1) * CJ, lanes]
                        src[k * 64 + x2 * COLS + z2 * 4 + y2] = jnp.concatenate([a, b], axis=1)
            for dx, dy in IN_PLANE:
                for k in range(2):
                    send(t, 1, k, xs[dx], z2 * 4 + ys[dy], (dx, dz, dy) == (0, 0, 0))

    def finish(t):
        back = recvs[t][1]

        zero = jnp.zeros((JH, 128), F32)

        def total(i, acc):
            return tuple(a + back[4 * i + n].astype(F32) for n, a in enumerate(acc))

        acc = lax.fori_loop(0, DEVICES // 4, total, (zero,) * 4, unroll=4)
        mean = ((acc[0] + acc[1]) + (acc[2] + acc[3])) * (1.0 / DEVICES)

        def square(i, acc):
            new = []
            for n, a in enumerate(acc):
                h = 4 * i + n
                d = back[h].astype(F32) - mean
                gbuf[pl.ds(pl.multiple_of(h * JH, JH), JH), :] = d
                new.append(a + d * d)
            return tuple(new)

        acc = lax.fori_loop(0, DEVICES // 4, square, (zero,) * 4, unroll=4)
        var = ((acc[0] + acc[1]) + (acc[2] + acc[3])) * (1.0 / DEVICES)
        rstd = lax.rsqrt(var + EPS)
        for j in range(JH):
            sl = slice(j * 128, (j + 1) * 128)
            tn = gbuf[pl.ds(j, DEVICES, stride=JH), :].astype(BF16)
            update = jnp.dot(wot[t], tn, preferred_element_type=F32)
            new = (pt[:, sl] + gate[:, sl] * (rstd[j : j + 1] * update)).astype(BF16).astype(F32)
            if t == 0:
                pt[:, sl] = new
                nt[:, sl] = norm_rows(new).astype(BF16)
            else:
                back_t = new.T
                xf[pl.ds(j, RI, stride=CJ), :] = back_t[:RI]
                xf[pl.ds(j + JH, RI, stride=CJ), :] = back_t[RI:]

    loads[0].wait()
    xf[...] = pair_ref[...].reshape(TOK, C).astype(F32)
    for j in range(JH):
        sl = slice(j * 128, (j + 1) * 128)
        tokens = jnp.concatenate(
            [xf[pl.ds(j, RI, stride=CJ), :], xf[pl.ds(j + JH, RI, stride=CJ), :]], axis=0
        )
        v = tokens.T
        pt[:, sl] = v
        nt[:, sl] = norm_rows(v).astype(BF16)
    for load in loads[1:]:
        load.wait()
    prepare_weights(0)
    project(0, 0, 0)
    pl.semaphore_wait(barrier, DEVICES - 1)
    for t in range(2):
        for k in range(2):
            for half in range(2):
                if (t, k, half) != (0, 0, 0):
                    project(t, k, half)
            for dx, dz, dy in FAR_FIRST:
                send(t, 0, k, xs[dx], cols[dz, dy], (dx, dz, dy) == (0, 0, 0))
        gates_of(t)
        if t == 0:
            prepare_weights(1)
        wait_arrived(t, 0)
        triangle_and_send(t)
        wait_arrived(t, 1)
        finish(t)
        for what in range(2):
            wait_sent(t, what, 1 - core)
    out_ref[...] = xf[...].astype(BF16).reshape(RI, CJ, C)


def on_device(pair_in, proj_weight, gate_weight, out_weight, block_mask):
    lr = pltpu.VMEM((DEVICES, 2, JH, 128), BF16)
    tr = pltpu.VMEM((DEVICES, JH, 128), BF16)
    vmem = pl.BlockSpec(memory_space=pltpu.VMEM)
    hbm = pl.BlockSpec(memory_space=pl.ANY)
    return pl.pallas_call(
        kernel,
        out_shape=jax.ShapeDtypeStruct((RI, CJ, C), BF16),
        in_specs=[hbm, hbm, hbm, hbm, pl.BlockSpec(memory_space=pltpu.SMEM)],
        out_specs=vmem,
        scratch_shapes=[
            pltpu.VMEM(pair_in.shape, BF16),
            pltpu.VMEM(proj_weight.shape, BF16),
            pltpu.VMEM(gate_weight.shape, BF16),
            pltpu.VMEM(out_weight.shape, BF16),
            pltpu.VMEM((TOK, C), F32),
            pltpu.VMEM((C, TOK), F32),
            pltpu.VMEM((C, TOK), BF16),
            pltpu.VMEM((C, TOK), F32),
            pltpu.VMEM((DEVICES // PLANE, 4 * PLANE, C), BF16),
            pltpu.VMEM((C, C), BF16),
            pltpu.VMEM((2, C, C), BF16),
            pltpu.VMEM((4 * PLANE * JH, 128), F32),
            pltpu.VMEM((DEVICES * JH, 128), F32),
            pltpu.VMEM((2, 4, N, 128), BF16),
            lr, lr, lr, lr, tr, tr, tr, tr,
            pltpu.SemaphoreType.DMA((2, 2, 2)),
            pltpu.SemaphoreType.DMA((2, 2)),
            pltpu.SemaphoreType.DMA((4,)),
        ],
        compiler_params=pltpu.CompilerParams(
            collective_id=0, has_side_effects=True, vmem_limit_bytes=60 * 2**20
        ),
        name="triangle_pair",
    )(pair_in, proj_weight, gate_weight, out_weight, block_mask)


def solution(mesh):
    placed = (P("row", "col", None), P(), P(), P(), P())
    return jax.shard_map(
        on_device, mesh=mesh, in_specs=placed, out_specs=P("row", "col", None), check_vma=False
    )
```

time: 66.9 us -> 62.3 us (0.931)
  Pallas kernels: 64.9 us -> 60.2 us
    pallas_call x1, Pallas kernels: 64.9 us -> 60.2 us  [on_device(): pl.pallas_call(kernel, out_shape=jax.ShapeDtypeStruct((RI, CJ, C), BF16),...]
where the time goes in v2:
time: 62.3 us; the launch traced here: 62.1 us
  Pallas kernels  60.2 us (97%)
  local copies, waits for them, and re-layouts  1.87 us (3%)
    pallas_call x1, Pallas kernels, on_device(): pl.pallas_call(kernel, out_shape=jax.ShapeDtypeStruct((RI, CJ, C), BF16),...  60.2 us
    unnamed x1, local copies, waits for them, and re-layouts  1.87 us

profile of v2, /device:TPU:1, one launch (start us, length us, event | category | flops | bytes accessed | tf_op | source)
XLA Modules:
  0.0 62.1 jit_solution(17862225512651658420)
XLA Ops:
  0.0 60.2 %triangle_pair.1 = bf16[64,32,128]{2,1,0:T(8,128)(2,1)} custom-call(bf16[64,32,128]{2,1,0:T(8,128)(2,1)} %pair_hbm.1, bf16[2,128,512]{2,1,0:T(8,128)(2,1)} %wp_hbm.1, bf16[2,128,128]{2,1,0:T(8,128)(2,1)} %wg_hbm.1, bf16[2,128,128]{2,1,0:T(8,128)(2,1)} %wo_hbm.1, s32[4,4]{1,0:T(4,128)} %mask_ref.1), custom_call_target="tpu_custom_call" | custom-call | tf_op jit(solution)/shard_map/triangle_pair/pallas_call | solution.py:267
  60.2 1.9 %copy.7 = bf16[64,32,128]{2,1,0:T(8,128)(2,1)} copy(bf16[64,32,128]{2,1,0:T(8,128)(2,1)} %triangle_pair.1) | data formatting | bytes 1048576

commit v3 on v2

--- a/solution.py
+++ b/solution.py
@@ -53,9 +53,9 @@
 
 
 def kernel(
-    pair_hbm, wp_hbm, wg_hbm, wo_hbm, mask_ref, out_ref,
-    pair_ref, wp_ref, wg_ref, wo_ref,
-    xf, pt, nt, gate, wpt, wgt, wot, fbuf, gbuf, mat,
+    pair_hbm, wp_hbm, wg_hbm, wo_hbm, mask_hbm, out_ref,
+    pair_ref, wp_ref, wg_ref, wo_ref, mask_ref,
+    xf, pt, nt, gate, wpt, wgt, wot, wsum, upd, fbuf, gbuf, mat,
     s_lr0, s_lr1, r_lr0, r_lr1, s_t0, s_t1, r_t0, r_t1,
     send_sem, recv_sem, load_sem,
 ):
@@ -63,7 +63,7 @@
     loads = [
         pltpu.make_async_copy(src, dst, load_sem.at[i])
         for i, (src, dst) in enumerate(
-            [(pair_hbm, pair_ref), (wp_hbm, wp_ref), (wg_hbm, wg_ref), (wo_hbm, wo_ref)]
+            [(pair_hbm, pair_ref), (mask_hbm, mask_ref), (wp_hbm, wp_ref), (wg_hbm, wg_ref), (wo_hbm, wo_ref)]
         )
     ]
     for load in loads:
@@ -84,7 +84,6 @@
                 there = {"row": row2, "col": cols[dz, dy]}
                 pl.semaphore_signal(barrier, inc=1, device_id=there, device_id_type=MESH)
 
-    mask = mask_ref[x, z].astype(F32)
     sends = ((s_lr0, s_t0), (s_lr1, s_t1))
     recvs = ((r_lr0, r_t0), (r_lr1, r_t1))
 
@@ -95,15 +94,16 @@
                 wpt[g, kind * PLANE : (kind + 1) * PLANE, :] = w[g * PLANE : (g + 1) * PLANE]
         wgt[...] = wg_ref[t].astype(F32).T.astype(BF16)
         wot[t] = wo_ref[t].astype(F32).T.astype(BF16)
-
-    def send(t, what, k, x2, c2, own):
+        wsum[t] = jnp.broadcast_to(jnp.sum(wot[t].astype(F32), axis=1, keepdims=True), (C, 128))
+
+    def send(t, what, k, x2, c2, own, arrival):
         src, land = sends[t][what], recvs[t][what]
         slot = k * 64 + x2 * COLS + c2
         copy = pltpu.make_async_remote_copy(
             src_ref=src.at[slot],
             dst_ref=land.at[me],
             send_sem=send_sem.at[t, what, k],
-            recv_sem=recv_sem.at[t, what],
+            recv_sem=recv_sem.at[t, what, arrival],
             device_id={"row": 2 * x2 + k, "col": c2},
             device_id_type=MESH,
         )
@@ -118,10 +118,19 @@
         src = sends[t][what].at[pl.ds(0, 64)]
         pltpu.make_async_copy(src, src, send_sem.at[t, what, k]).wait()
 
-    def wait_arrived(t, what):
-        wait_sent(t, what, core)
-        land = recvs[t][what].at[pl.ds(0, DEVICES - 1)]
-        pltpu.make_async_copy(land, land, recv_sem.at[t, what]).wait()
+    def wait_tiles(t, what, count, arrival):
+        land = recvs[t][what].at[pl.ds(0, count)]
+        pltpu.make_async_copy(land, land, recv_sem.at[t, what, arrival]).wait()
+
+    def wait_triangle(t, k):
+        @pl.when(core == k)
+        def _():
+            wait_sent(t, 1, k)
+            wait_tiles(t, 1, 63, k)
+
+        @pl.when(core != k)
+        def _():
+            wait_tiles(t, 1, 64, k)
 
     halves = ((xs[2], xa), (xb, xs[0]))
 
@@ -158,17 +167,23 @@
         land = recvs[t][0]
         src = sends[t][1]
 
-        def relayout(c, carry):
-            rows = pl.ds(pl.multiple_of(c * CJ, CJ), JH), pl.ds(pl.multiple_of(c * CJ + JH, JH), JH)
-            for side in range(2):
-                for x2 in range(4):
-                    a = land[x2 * COLS + c, side]
-                    b = land[64 + x2 * COLS + c, side]
+        def relayout(offsets):
+            for dx, dz, dy in offsets:
+                x2, c = xs[dx], cols[dz, dy]
+                slot = x2 * COLS + c
+                rows = pl.ds(pl.multiple_of(c * CJ, CJ), JH), pl.ds(pl.multiple_of(c * CJ + JH, JH), JH)
+                for side in range(2):
+                    a, b = land[slot, side], land[64 + slot, side]
                     mat[side, x2, rows[0]] = jnp.concatenate([a[:, :64], b[:, :64]], axis=1)
                     mat[side, x2, rows[1]] = jnp.concatenate([a[:, 64:], b[:, 64:]], axis=1)
-            return carry
-
-        lax.fori_loop(0, COLS, relayout, 0, unroll=4)
+
+        far = [offset for offset in FAR_FIRST if hops(offset) >= 3]
+        near = [offset for offset in FAR_FIRST if hops(offset) < 3]
+        wait_tiles(t, 0, 2 * len(far), 0)
+        relayout(far)
+        wait_sent(t, 0, core)
+        wait_tiles(t, 0, 2 * len(near) - 1, 1)
+        relayout(near)
         left = jnp.concatenate([mat[0, x2] for x2 in range(4)], axis=1)
         for dz, z2 in ((2, zs[2]), (1, za), (3, zb), (0, zs[0])):
             if t == 0:
@@ -187,7 +202,7 @@
                         src[k * 64 + x2 * COLS + z2 * 4 + y2] = jnp.concatenate([a, b], axis=1)
             for dx, dy in IN_PLANE:
                 for k in range(2):
-                    send(t, 1, k, xs[dx], z2 * 4 + ys[dy], (dx, dz, dy) == (0, 0, 0))
+                    send(t, 1, k, xs[dx], z2 * 4 + ys[dy], (dx, dz, dy) == (0, 0, 0), core)
 
     def finish(t):
         back = recvs[t][1]
@@ -195,27 +210,51 @@
         zero = jnp.zeros((JH, 128), F32)
 
         def total(i, acc):
-            return tuple(a + back[4 * i + n].astype(F32) for n, a in enumerate(acc))
-
-        acc = lax.fori_loop(0, DEVICES // 4, total, (zero,) * 4, unroll=4)
-        mean = ((acc[0] + acc[1]) + (acc[2] + acc[3])) * (1.0 / DEVICES)
+            new = []
+            for n, a in enumerate(acc):
+                h = 4 * i + n
+                v = back[h].astype(F32)
+                gbuf[pl.ds(pl.multiple_of(h * JH, JH), JH), :] = v
+                new.append(a + v)
+            return tuple(new)
 
         def square(i, acc):
             new = []
             for n, a in enumerate(acc):
-                h = 4 * i + n
-                d = back[h].astype(F32) - mean
-                gbuf[pl.ds(pl.multiple_of(h * JH, JH), JH), :] = d
+                d = back[4 * i + n].astype(F32) - shift
                 new.append(a + d * d)
             return tuple(new)
 
-        acc = lax.fori_loop(0, DEVICES // 4, square, (zero,) * 4, unroll=4)
-        var = ((acc[0] + acc[1]) + (acc[2] + acc[3])) * (1.0 / DEVICES)
-        rstd = lax.rsqrt(var + EPS)
+        def both(i, acc):
+            new = []
+            for n in range(4):
+                h = 64 + 4 * i + n
+                v = back[h].astype(F32)
+                gbuf[pl.ds(pl.multiple_of(h * JH, JH), JH), :] = v
+                d = v - shift
+                new += [acc[2 * n] + d, acc[2 * n + 1] + d * d]
+            return tuple(new)
+
+        def product(j, k):
+            tn = gbuf[pl.ds(k * 64 * JH + j, 64, stride=JH), :].astype(BF16)
+            return jnp.dot(wot[t, :, k * 64 : (k + 1) * 64], tn, preferred_element_type=F32)
+
+        wait_triangle(t, 0)
+        acc = lax.fori_loop(0, 16, total, (zero,) * 4, unroll=4)
+        shift = ((acc[0] + acc[1]) + (acc[2] + acc[3])) * (1.0 / 64)
+        acc = lax.fori_loop(0, 16, square, (zero,) * 4, unroll=4)
+        below = (acc[0] + acc[1]) + (acc[2] + acc[3])
+        for j in range(JH):
+            upd[:, j * 128 : (j + 1) * 128] = product(j, 0)
+        wait_triangle(t, 1)
+        acc = lax.fori_loop(0, 16, both, (zero,) * 8, unroll=4)
+        delta = ((acc[0] + acc[2]) + (acc[4] + acc[6])) * (1.0 / DEVICES)
+        square_sum = below + ((acc[1] + acc[3]) + (acc[5] + acc[7]))
+        rstd = lax.rsqrt(square_sum * (1.0 / DEVICES) - delta * delta + EPS)
+        mean = shift + delta
         for j in range(JH):
             sl = slice(j * 128, (j + 1) * 128)
-            tn = gbuf[pl.ds(j, DEVICES, stride=JH), :].astype(BF16)
-            update = jnp.dot(wot[t], tn, preferred_element_type=F32)
+            update = upd[:, sl] + product(j, 1) - wsum[t] * mean[j : j + 1]
             new = (pt[:, sl] + gate[:, sl] * (rstd[j : j + 1] * update)).astype(BF16).astype(F32)
             if t == 0:
                 pt[:, sl] = new
@@ -237,6 +276,7 @@
         nt[:, sl] = norm_rows(v).astype(BF16)
     for load in loads[1:]:
         load.wait()
+    mask = mask_ref[x, z].astype(F32)
     prepare_weights(0)
     project(0, 0, 0)
     pl.semaphore_wait(barrier, DEVICES - 1)
@@ -246,13 +286,11 @@
                 if (t, k, half) != (0, 0, 0):
                     project(t, k, half)
             for dx, dz, dy in FAR_FIRST:
-                send(t, 0, k, xs[dx], cols[dz, dy], (dx, dz, dy) == (0, 0, 0))
+                send(t, 0, k, xs[dx], cols[dz, dy], (dx, dz, dy) == (0, 0, 0), int(hops((dx, dz, dy)) < 3))
         gates_of(t)
         if t == 0:
             prepare_weights(1)
-        wait_arrived(t, 0)
         triangle_and_send(t)
-        wait_arrived(t, 1)
         finish(t)
         for what in range(2):
             wait_sent(t, what, 1 - core)
@@ -263,17 +301,18 @@
     lr = pltpu.VMEM((DEVICES, 2, JH, 128), BF16)
     tr = pltpu.VMEM((DEVICES, JH, 128), BF16)
     vmem = pl.BlockSpec(memory_space=pltpu.VMEM)
-    hbm = pl.BlockSpec(memory_space=pl.ANY)
+    hbm = pl.BlockSpec(memory_space=pltpu.HBM)
     return pl.pallas_call(
         kernel,
         out_shape=jax.ShapeDtypeStruct((RI, CJ, C), BF16),
-        in_specs=[hbm, hbm, hbm, hbm, pl.BlockSpec(memory_space=pltpu.SMEM)],
+        in_specs=[hbm] * 5,
         out_specs=vmem,
         scratch_shapes=[
             pltpu.VMEM(pair_in.shape, BF16),
             pltpu.VMEM(proj_weight.shape, BF16),
             pltpu.VMEM(gate_weight.shape, BF16),
             pltpu.VMEM(out_weight.shape, BF16),
+            pltpu.SMEM(block_mask.shape, jnp.int32),
             pltpu.VMEM((TOK, C), F32),
             pltpu.VMEM((C, TOK), F32),
             pltpu.VMEM((C, TOK), BF16),
@@ -281,19 +320,21 @@
             pltpu.VMEM((DEVICES // PLANE, 4 * PLANE, C), BF16),
             pltpu.VMEM((C, C), BF16),
             pltpu.VMEM((2, C, C), BF16),
+            pltpu.VMEM((2, C, 128), F32),
+            pltpu.VMEM((C, TOK), F32),
             pltpu.VMEM((4 * PLANE * JH, 128), F32),
             pltpu.VMEM((DEVICES * JH, 128), F32),
             pltpu.VMEM((2, 4, N, 128), BF16),
             lr, lr, lr, lr, tr, tr, tr, tr,
             pltpu.SemaphoreType.DMA((2, 2, 2)),
-            pltpu.SemaphoreType.DMA((2, 2)),
-            pltpu.SemaphoreType.DMA((4,)),
+            pltpu.SemaphoreType.DMA((2, 2, 2)),
+            pltpu.SemaphoreType.DMA((5,)),
         ],
         compiler_params=pltpu.CompilerParams(
-            collective_id=0, has_side_effects=True, vmem_limit_bytes=60 * 2**20
+            collective_id=0, has_side_effects=True, vmem_limit_bytes=40 * 2**20
         ),
         name="triangle_pair",
-    )(pair_in, proj_weight, gate_weight, out_weight, block_mask)
+    )(*(pltpu.with_memory_space_constraint(v, pltpu.HBM) for v in (pair_in, proj_weight, gate_weight, out_weight, block_mask)))
 
 
 def solution(mesh):

time: 62.3 us -> 58.4 us (0.937)
  Pallas kernels: 60.2 us -> 57.5 us
  local copies, waits for them, and re-layouts: 1.87 us -> 0.8 us
    pallas_call x1, Pallas kernels: 60.2 us -> 57.5 us  [on_device(): pl.pallas_call(kernel, out_shape=jax.ShapeDtypeStruct((RI, CJ, C), BF16),...]
    unnamed x1, local copies, waits for them, and re-layouts: 1.87 us -> 0.8 us
where the time goes in v3:
time: 58.4 us; the launch traced here: 58.3 us
  Pallas kernels  57.5 us (98%)
  local copies, waits for them, and re-layouts  0.8 us (1%)
    pallas_call x1, Pallas kernels, on_device(): pl.pallas_call(kernel, out_shape=jax.ShapeDtypeStruct((RI, CJ, C), BF16),...  57.5 us

profile of v3, /device:TPU:1, one launch (start us, length us, event | category | flops | bytes accessed | tf_op | source)
XLA Modules:
  0.0 58.3 jit_solution(15949935972881042978)
XLA Ops:
  0.0 57.5 %triangle_pair.1 = bf16[64,32,128]{2,1,0:T(8,128)(2,1)S(1)} custom-call(bf16[64,32,128]{2,1,0:T(8,128)(2,1)} %pair_hbm.1, bf16[2,128,512]{2,1,0:T(8,128)(2,1)} %wp_hbm.1, bf16[2,128,128]{2,1,0:T(8,128)(2,1)} %wg_hbm.1, bf16[2,128,128]{2,1,0:T(8,128)(2,1)} %wo_hbm.1, s32[4,4]{1,0:T(4,128)} %mask_hbm.1), custom_call_target="tpu_custom_call" | custom-call | tf_op jit(solution)/shard_map/triangle_pair/pallas_call | solution.py:305
  57.5 0.8 %copy.7 = bf16[64,32,128]{2,1,0:T(8,128)(2,1)} copy(bf16[64,32,128]{2,1,0:T(8,128)(2,1)S(1)} %triangle_pair.1) | data formatting | bytes 1048576

commit v4 on v3

--- a/solution.py
+++ b/solution.py
@@ -17,6 +17,8 @@
 RI, CJ = 64, 32
 JH = 16
 TOK = RI * CJ
+JP = 24
+XP = 40
 PLANE = COLS
 
 
@@ -136,7 +138,7 @@
 
     def project(t, k, half):
         src = sends[t][0]
-        size = PLANE * JH
+        size = PLANE * JP
         planes = halves[half]
         w = jnp.concatenate([wpt[k * 4 + x2] for x2 in planes], axis=0)
         for q in range(TOK // 256):
@@ -147,12 +149,13 @@
                     proj = mask * sigmoid(v[at + PLANE : at + 2 * PLANE]) * v[at : at + PLANE]
                     for half in range(2):
                         to = (2 * p + side) * size + 2 * q + half
-                        fbuf[pl.ds(to, PLANE, stride=JH), :] = proj[:, half * 128 : (half + 1) * 128]
+                        fbuf[pl.ds(to, PLANE, stride=JP), :] = proj[:, half * 128 : (half + 1) * 128]
         for p in range(2):
             for side in range(2):
                 at = (2 * p + side) * size
-                tiles = fbuf[at : at + size, :].astype(BF16).reshape(PLANE, JH, 128)
-                src[pl.ds(k * 64 + planes[p] * COLS, PLANE), side] = tiles
+                for h in range(PLANE):
+                    tile = fbuf[at + h * JP : at + h * JP + JH, :].astype(BF16)
+                    src[k * 64 + planes[p] * COLS + h, side] = tile
 
     def send_half(t, k, half):
         for p, dz, dy in HALVES[half]:
@@ -214,7 +217,7 @@
             for n, a in enumerate(acc):
                 h = 4 * i + n
                 v = back[h].astype(F32)
-                gbuf[pl.ds(pl.multiple_of(h * JH, JH), JH), :] = v
+                gbuf[pl.ds(pl.multiple_of(h * JP, 8), JH), :] = v
                 new.append(a + v)
             return tuple(new)
 
@@ -230,13 +233,13 @@
             for n in range(4):
                 h = 64 + 4 * i + n
                 v = back[h].astype(F32)
-                gbuf[pl.ds(pl.multiple_of(h * JH, JH), JH), :] = v
+                gbuf[pl.ds(pl.multiple_of(h * JP, 8), JH), :] = v
                 d = v - shift
                 new += [acc[2 * n] + d, acc[2 * n + 1] + d * d]
             return tuple(new)
 
         def product(j, k):
-            tn = gbuf[pl.ds(k * 64 * JH + j, 64, stride=JH), :].astype(BF16)
+            tn = gbuf[pl.ds(k * 64 * JP + j, 64, stride=JP), :].astype(BF16)
             return jnp.dot(wot[t, :, k * 64 : (k + 1) * 64], tn, preferred_element_type=F32)
 
         wait_triangle(t, 0)
@@ -261,15 +264,16 @@
                 nt[:, sl] = norm_rows(new).astype(BF16)
             else:
                 back_t = new.T
-                xf[pl.ds(j, RI, stride=CJ), :] = back_t[:RI]
-                xf[pl.ds(j + JH, RI, stride=CJ), :] = back_t[RI:]
+                xf[pl.ds(j, RI, stride=XP), :] = back_t[:RI]
+                xf[pl.ds(j + JH, RI, stride=XP), :] = back_t[RI:]
 
     loads[0].wait()
-    xf[...] = pair_ref[...].reshape(TOK, C).astype(F32)
+    for i in range(RI):
+        xf[i * XP : i * XP + CJ, :] = pair_ref[i].astype(F32)
     for j in range(JH):
         sl = slice(j * 128, (j + 1) * 128)
         tokens = jnp.concatenate(
-            [xf[pl.ds(j, RI, stride=CJ), :], xf[pl.ds(j + JH, RI, stride=CJ), :]], axis=0
+            [xf[pl.ds(j, RI, stride=XP), :], xf[pl.ds(j + JH, RI, stride=XP), :]], axis=0
         )
         v = tokens.T
         pt[:, sl] = v
@@ -294,7 +298,8 @@
         finish(t)
         for what in range(2):
             wait_sent(t, what, 1 - core)
-    out_ref[...] = xf[...].astype(BF16).reshape(RI, CJ, C)
+    for i in range(RI):
+        out_ref[i] = xf[i * XP : i * XP + CJ, :].astype(BF16)
 
 
 def on_device(pair_in, proj_weight, gate_weight, out_weight, block_mask):
@@ -313,7 +318,7 @@
             pltpu.VMEM(gate_weight.shape, BF16),
             pltpu.VMEM(out_weight.shape, BF16),
             pltpu.SMEM(block_mask.shape, jnp.int32),
-            pltpu.VMEM((TOK, C), F32),
+            pltpu.VMEM((RI * XP, C), F32),
             pltpu.VMEM((C, TOK), F32),
             pltpu.VMEM((C, TOK), BF16),
             pltpu.VMEM((C, TOK), F32),
@@ -322,8 +327,8 @@
             pltpu.VMEM((2, C, C), BF16),
             pltpu.VMEM((2, C, 128), F32),
             pltpu.VMEM((C, TOK), F32),
-            pltpu.VMEM((4 * PLANE * JH, 128), F32),
-            pltpu.VMEM((DEVICES * JH, 128), F32),
+            pltpu.VMEM((4 * PLANE * JP, 128), F32),
+            pltpu.VMEM((DEVICES * JP, 128), F32),
             pltpu.VMEM((2, 4, N, 128), BF16),
             lr, lr, lr, lr, tr, tr, tr, tr,
             pltpu.SemaphoreType.DMA((2, 2, 2)),

time: 58.4 us -> 57.7 us (0.988)
  Pallas kernels: 57.5 us -> 56.8 us
    pallas_call x1, Pallas kernels: 57.5 us -> 56.8 us  [on_device(): pl.pallas_call(kernel, out_shape=jax.ShapeDtypeStruct((RI, CJ, C), BF16),...]
where the time goes in v4:
time: 57.7 us; the launch traced here: 57.6 us
  Pallas kernels  56.8 us (98%)
  local copies, waits for them, and re-layouts  0.8 us (1%)
    pallas_call x1, Pallas kernels, on_device(): pl.pallas_call(kernel, out_shape=jax.ShapeDtypeStruct((RI, CJ, C), BF16),...  56.8 us

profile of v4, /device:TPU:1, one launch (start us, length us, event | category | flops | bytes accessed | tf_op | source)
XLA Modules:
  0.0 57.6 jit_solution(15883274155891252393)
XLA Ops:
  0.0 56.8 %triangle_pair.1 = bf16[64,32,128]{2,1,0:T(8,128)(2,1)S(1)} custom-call(bf16[64,32,128]{2,1,0:T(8,128)(2,1)} %pair_hbm.1, bf16[2,128,512]{2,1,0:T(8,128)(2,1)} %wp_hbm.1, bf16[2,128,128]{2,1,0:T(8,128)(2,1)} %wg_hbm.1, bf16[2,128,128]{2,1,0:T(8,128)(2,1)} %wo_hbm.1, s32[4,4]{1,0:T(4,128)} %mask_hbm.1), custom_call_target="tpu_custom_call" | custom-call | tf_op jit(solution)/shard_map/triangle_pair/pallas_call | solution.py:310
  56.8 0.8 %copy.7 = bf16[64,32,128]{2,1,0:T(8,128)(2,1)} copy(bf16[64,32,128]{2,1,0:T(8,128)(2,1)S(1)} %triangle_pair.1) | data formatting | bytes 1048576

commit v5 on v4

--- a/solution.py
+++ b/solution.py
@@ -239,7 +239,9 @@
             return tuple(new)
 
         def product(j, k):
-            tn = gbuf[pl.ds(k * 64 * JP + j, 64, stride=JP), :].astype(BF16)
+            tn = jnp.concatenate(
+                [gbuf[pl.ds(k * 64 * JP + n, 64, stride=JP), :].astype(BF16) for n in (j, j + 1)], axis=1
+            )
             return jnp.dot(wot[t, :, k * 64 : (k + 1) * 64], tn, preferred_element_type=F32)
 
         wait_triangle(t, 0)
@@ -247,8 +249,8 @@
         shift = ((acc[0] + acc[1]) + (acc[2] + acc[3])) * (1.0 / 64)
         acc = lax.fori_loop(0, 16, square, (zero,) * 4, unroll=4)
         below = (acc[0] + acc[1]) + (acc[2] + acc[3])
-        for j in range(JH):
-            upd[:, j * 128 : (j + 1) * 128] = product(j, 0)
+        for j in range(0, JH, 2):
+            upd[:, j * 128 : (j + 2) * 128] = product(j, 0)
         wait_triangle(t, 1)
         acc = lax.fori_loop(0, 16, both, (zero,) * 8, unroll=4)
         delta = ((acc[0] + acc[2]) + (acc[4] + acc[6])) * (1.0 / DEVICES)
@@ -257,7 +259,9 @@
         mean = shift + delta
         for j in range(JH):
             sl = slice(j * 128, (j + 1) * 128)
-            update = upd[:, sl] + product(j, 1) - wsum[t] * mean[j : j + 1]
+            if j % 2 == 0:
+                pair = product(j, 1)
+            update = upd[:, sl] + pair[:, j % 2 * 128 : (j % 2 + 1) * 128] - wsum[t] * mean[j : j + 1]
             new = (pt[:, sl] + gate[:, sl] * (rstd[j : j + 1] * update)).astype(BF16).astype(F32)
             if t == 0:
                 pt[:, sl] = new

time: 57.7 us -> 57.6 us (level)
  no operation moved by 1% of the time
where the time goes in v5:
time: 57.6 us; the launch traced here: 57.5 us
  Pallas kernels  56.7 us (98%)
  local copies, waits for them, and re-layouts  0.8 us (1%)
    pallas_call x1, Pallas kernels, on_device(): pl.pallas_call(kernel, out_shape=jax.ShapeDtypeStruct((RI, CJ, C), BF16),...  56.7 us

profile of v5, /device:TPU:1, one launch (start us, length us, event | category | flops | bytes accessed | tf_op | source)
XLA Modules:
  0.0 57.5 jit_solution(10179053269374338170)
XLA Ops:
  0.0 56.7 %triangle_pair.1 = bf16[64,32,128]{2,1,0:T(8,128)(2,1)S(1)} custom-call(bf16[64,32,128]{2,1,0:T(8,128)(2,1)} %pair_hbm.1, bf16[2,128,512]{2,1,0:T(8,128)(2,1)} %wp_hbm.1, bf16[2,128,128]{2,1,0:T(8,128)(2,1)} %wg_hbm.1, bf16[2,128,128]{2,1,0:T(8,128)(2,1)} %wo_hbm.1, s32[4,4]{1,0:T(4,128)} %mask_hbm.1), custom_call_target="tpu_custom_call" | custom-call | tf_op jit(solution)/shard_map/triangle_pair/pallas_call | solution.py:314
  56.7 0.8 %copy.7 = bf16[64,32,128]{2,1,0:T(8,128)(2,1)} copy(bf16[64,32,128]{2,1,0:T(8,128)(2,1)S(1)} %triangle_pair.1) | data formatting | bytes 1048576
